TPU v7x, 32 devices: a whole 2x2x4 slice. The times are simulated.
32 devices in a mesh: atom: 2 (over x), slab: 16 (over z, y, core).
Axes of the slice: x: 2, y: 2, z: 4, core: 2. Of those that a mesh axis runs over, the one named last changes fastest.
Arguments:
- atom_log_density: float32 [2, 256, 64, 512], P('atom', 'slab'), may hold values from -123 to 121
- prior_log_scaling: float32 [2, 256, 64, 512], P('atom', 'slab'), may hold values from -5 to 115
- atom_cotangent_rows: float32 [2, 256, 64, 512], P('atom', 'slab'), may hold values from -6 to 6
- barycenter_cotangent: float32 [256, 64, 512], P('slab'), may hold values from -6 to 6
- weights: float32 [2], replicated, may hold values from 0.2 to 1
- band: int32 [3], replicated, may hold values from 1 to 8, as said below
- slot_atom_index: int32 [2], replicated, may hold values from 0 to 1, each once
Outputs:
- log_atom_gradient: float32 [2, 256, 64, 512], P('atom', 'slab')
- weight_grad: float32 [2], replicated
Inputs may be any that keep to these rules, and one draw needn't show every extreme that they name: `band`: at least one entry equals 8. `slot_atom_index`: each atom is held in exactly one slot.
All inputs are finite; a program needn't handle non-finite values.
Results may differ from a plain program's by a relative error of at most 0.0003.
Values sent between devices are 32-bit elements; how exact they have to be, the bound alone decides.
A program may use at most 64 MiB of HBM per device.

v0:
```python
import jax
import jax.numpy as jnp
from jax import lax
from jax.sharding import PartitionSpec as P

BAND_MAX = 8


def kernel_table(row_count, col_count, half):
    row_pos = jnp.arange(row_count, dtype=jnp.int32)
    col_pos = jnp.arange(col_count, dtype=jnp.int32)
    offsets = row_pos[:, None] - col_pos[None, :]
    spread = offsets.astype(jnp.float32)
    values = jnp.exp(-2.0 * spread * spread / (BAND_MAX * BAND_MAX))
    return jnp.where(jnp.abs(offsets) <= half, values, jnp.float32(0.0))


def gaussian_blur_slabs(field, kernel_columns, kernel_rows, band):
    high = lax.Precision.HIGHEST
    section = jnp.einsum("azyx,xv->azyv", field, kernel_columns, precision=high)
    section = jnp.einsum("azyx,yv->azvx", section, kernel_rows, precision=high)
    plane_count = field.shape[1]
    all_planes = plane_count * lax.axis_size("slab")
    kern_z = kernel_table(all_planes, all_planes, band[2])
    blurred = jnp.einsum(
        "pq,aqyx->apyx",
        kern_z,
        lax.all_to_all(section, "slab", split_axis=2, concat_axis=1, tiled=True),
        precision=high,
    )
    return lax.all_to_all(blurred, "slab", split_axis=1, concat_axis=2, tiled=True)


def body(
    atom_log_density,
    prior_log_scaling,
    atom_cotangent_rows,
    barycenter_cotangent,
    weights,
    band,
    slot_atom_index,
):
    held = atom_log_density.shape[0]
    plane_count, row_count, col_count = barycenter_cotangent.shape
    all_cells = plane_count * lax.axis_size("slab") * row_count * col_count
    kernel_columns = kernel_table(col_count, col_count, band[0])
    kernel_rows = kernel_table(row_count, row_count, band[1])
    atom_start = lax.axis_index("atom") * held
    slot_ids = lax.dynamic_slice_in_dim(slot_atom_index, atom_start, held)
    onehot = (slot_ids[:, None] == jnp.arange(weights.shape[0], dtype=jnp.int32)[None, :]).astype(
        jnp.float32
    )
    weight_here = jnp.sum(onehot * weights[None, :], axis=1)
    summed = barycenter_cotangent + lax.psum(jnp.sum(atom_cotangent_rows, axis=0), "atom")
    peak_gradient = lax.pmax(jnp.max(prior_log_scaling, axis=(1, 2, 3)), "slab")
    first_entry = gaussian_blur_slabs(
        jnp.exp(prior_log_scaling - peak_gradient[:, None, None, None]),
        kernel_columns,
        kernel_rows,
        band,
    )
    potential = atom_log_density - (jnp.log(first_entry) + peak_gradient[:, None, None, None])
    peak_f = lax.pmax(jnp.max(potential, axis=(1, 2, 3)), "slab")
    shifted = jnp.exp(potential - peak_f[:, None, None, None])
    second = gaussian_blur_slabs(shifted, kernel_columns, kernel_rows, band)
    mixed = jnp.log(second) + peak_f[:, None, None, None]
    adjoint = weight_here[:, None, None, None] * summed[None] - atom_cotangent_rows
    log_atom_gradient = shifted * gaussian_blur_slabs(
        adjoint / second, kernel_columns, kernel_rows, band
    )
    partial_value = jnp.sum(summed[None] * mixed, axis=(1, 2, 3))
    spread_sums = jnp.sum(onehot * partial_value[:, None], axis=0)
    weight_grad = lax.psum(spread_sums, ("atom", "slab")) / all_cells
    return (log_atom_gradient, weight_grad)


def solution(mesh):
    return jax.shard_map(
        body,
        mesh=mesh,
        in_specs=(
            P("atom", "slab", None, None),
            P("atom", "slab", None, None),
            P("atom", "slab", None, None),
            P("slab", None, None),
            P(),
            P(),
            P(),
        ),
        out_specs=(P("atom", "slab", None, None), P()),
        check_vma=False,
    )
```

profile of v0, /device:TPU:0, one launch (start us, length us, event | category | flops | bytes accessed | tf_op | source)
XLA Modules:
  0.0 518.5 jit_solution(4078364188520569177)
XLA Ops:
  7.2 2.9 reduce_max.22
  10.1 35.5 %pmax.14 = f32[]{:T(128)} all-reduce(f32[]{:T(128)} %reduce_max.22), channel_id=1, replica_groups=mesh['atom'=2,'slab'=16] {'slab'}, use_global_device_ids=true, to_apply=%region_1.2 | all-reduce | flops 1 | bytes 8 | tf_op jit(solution)/shard_map/pmax | solution.py:55
  46.2 5.4 %fusion.3 = f32[16,64,512]{2,1,0:T(8,128)S(1)} fusion(f32[1,16,64,512]{3,2,1,0:T(8,128)S(1)} %copy-done.5, f32[]{:T(128)} %pmax.14, s32[]{:T(128)} %bitcast.3), kind=kOutput, calls=%fused_computation.5 | convolution fusion | flops 3223846912 | bytes 4194312 | tf_op jit(solution)/shard_map/azyx,xv->azyv/dot_general | solution.py:20
  55.4 49.9 %all_to_all.90 = f32[1,16,64,512]{3,1,0,2:T(8,128)S(1)} all-to-all(f32[1,16,64,512]{3,1,0,2:T(8,128)S(1)} %copy.68), channel_id=1, replica_groups=mesh['atom'=2,'slab'=16] {'slab'}, dimensions={2} | all-to-all | bytes 4194304 | tf_op jit(solution)/shard_map/all_to_all | solution.py:28
  105.6 5.4 %convolution_bitcast_fusion.5 = f32[1,256,4,512]{1,3,2,0:T(8,128)} fusion(f32[256,4,512]{2,0,1:T(8,128)S(1)} %bitcast.99, s32[]{:T(128)} %bitcast.10), kind=kOutput, calls=%fused_computation.27 | convolution fusion | flops 1611137024 | bytes 4194308 | tf_op jit(solution)/shard_map/pq,aqyx->apyx/dot_general | solution.py:25
  111.0 3.1 copy.71
  114.1 52.7 %all_to_all.91 = f32[1,256,4,512]{3,2,0,1:T(4,128)S(1)} all-to-all(f32[1,256,4,512]{3,2,0,1:T(4,128)} %copy.71), channel_id=1, replica_groups=mesh['atom'=2,'slab'=16] {'slab'}, dimensions={1} | all-to-all | bytes 4194304 | tf_op jit(solution)/shard_map/all_to_all | solution.py:31
  171.7 33.7 %pmax.15 = f32[]{:T(128)} all-reduce(f32[]{:T(128)} %fusion.100), channel_id=1, replica_groups=mesh['atom'=2,'slab'=16] {'slab'}, use_global_device_ids=true, to_apply=%region_3.4 | all-reduce | flops 1 | bytes 8 | tf_op jit(solution)/shard_map/pmax | solution.py:63
  205.4 3.6 fusion.13
  209.0 5.4 %fusion.7 = f32[16,64,512]{2,1,0:T(8,128)S(1)} fusion(f32[16,64,512]{2,0,1:T(8,128)S(1)} %fusion.13, s32[]{:T(128)} %bitcast.3), kind=kOutput, calls=%fused_computation.9 | convolution fusion | flops 3223322624 | bytes 4194308 | tf_op jit(solution)/shard_map/azyx,xv->azyv/dot_general | solution.py:20
  218.2 49.9 %all_to_all.92 = f32[1,16,64,512]{3,1,0,2:T(8,128)S(1)} all-to-all(f32[1,16,64,512]{3,1,0,2:T(8,128)S(1)} %copy.79), channel_id=1, replica_groups=mesh['atom'=2,'slab'=16] {'slab'}, dimensions={2} | all-to-all | bytes 4194304 | tf_op jit(solution)/shard_map/all_to_all | solution.py:28
  268.5 5.6 %convolution_bitcast_fusion.4 = f32[1,256,4,512]{1,3,2,0:T(8,128)} fusion(f32[256,4,512]{2,0,1:T(8,128)S(1)} %bitcast.104, s32[]{:T(128)} %bitcast.10), kind=kOutput, calls=%fused_computation.26 | convolution fusion | flops 1611137024 | bytes 4194308 | tf_op jit(solution)/shard_map/pq,aqyx->apyx/dot_general | solution.py:25
  274.1 3.0 copy.82
  277.1 5.0 all-to-all-start.3
  282.3 4.1 copy.118
  288.9 34.3 %all-to-all-done.3 = f32[1,256,4,512]{3,2,0,1:T(4,128)} async-done(((f32[1,256,4,512]{3,2,0,1:T(4,128)}), f32[1,256,4,512]{3,2,0,1:T(4,128)}, u32[]{:S(2)}, u32[]{:S(2)}) %all-to-all-start.3) | async-done | bytes 2097184 | tf_op jit(solution)/shard_map/all_to_all | solution.py:31
  328.5 22.4 %all-reduce.2.cloned.1.call-done = f32[16,64,512]{2,0,1:T(8,128)} async-done(((f32[16,64,512]{2,0,1:T(8,128)}), f32[16,64,512]{2,0,1:T(8,128)}) %all-reduce.2.cloned.1.call-update) | async-done | bytes 2097168 | tf_op jit(solution)/shard_map/psum | solution.py:54
  350.8 6.8 %fusion.2 = f32[16,64,512]{2,0,1:T(8,128)S(1)} fusion(f32[1,16,64,512]{3,1,2,0:T(8,128)} %bitcast.107, f32[1,16,64,512]{3,2,1,0:T(8,128)} %param.9, f32[]{:T(128)} %fusion.72, f32[16,64,512]{2,0,1:T(8,128)} %all-reduce.2.cloned.1.call-done, f32[16,64,512]{2,1,0:T(8,128)} %param.10), kind=kLoop, calls=%fused_computation.4 | loop fusion | flops 2097152 | bytes 10485764 | tf_op jit(solution)/shard_map/reshape.19
  357.6 5.4 %fusion.5 = f32[16,64,512]{2,1,0:T(8,128)S(1)} fusion(f32[16,64,512]{2,0,1:T(8,128)S(1)} %fusion.2, s32[]{:T(128)} %bitcast.3), kind=kOutput, calls=%fused_computation.7 | convolution fusion | flops 3223322624 | bytes 4194308 | tf_op jit(solution)/shard_map/azyx,xv->azyv/dot_general | solution.py:20
  367.1 52.7 %all_to_all.93 = f32[1,16,64,512]{3,1,0,2:T(8,128)S(1)} all-to-all(f32[1,16,64,512]{3,1,0,2:T(8,128)S(1)} %copy.86), channel_id=1, replica_groups=mesh['atom'=2,'slab'=16] {'slab'}, dimensions={2} | all-to-all | bytes 4194304 | tf_op jit(solution)/shard_map/all_to_all | solution.py:28
  420.1 5.6 %convolution_bitcast_fusion.3 = f32[1,256,4,512]{1,3,2,0:T(8,128)} fusion(f32[256,4,512]{2,0,1:T(8,128)S(1)} %bitcast.101, s32[]{:T(128)} %bitcast.10), kind=kOutput, calls=%fused_computation.25 | convolution fusion | flops 1611137024 | bytes 4194308 | tf_op jit(solution)/shard_map/pq,aqyx->apyx/dot_general | solution.py:25
  425.7 3.0 copy.89
  428.8 5.2 all-to-all-start.5
  442.1 60.2 %psum.15 = f32[2]{0:T(128)S(1)} all-reduce(f32[2]{0:T(128)S(1)} %compare_select_fusion), channel_id=1, replica_groups=mesh['atom'=2,'slab'=16] {'atom','slab'}, use_global_device_ids=true, to_apply=%region_7.8 | all-reduce | flops 2 | bytes 16 | tf_op jit(solution)/shard_map/psum | solution.py:73
  (47 shorter events, 43.1 us)
Async XLA Ops:
  7.2 39.1 %copy-start.5 = (f32[1,16,64,512]{3,2,1,0:T(8,128)S(1)}, f32[1,16,64,512]{3,2,1,0:T(8,128)}, u32[]{:S(2)}) copy-start(f32[1,16,64,512]{3,2,1,0:T(8,128)} %param.8) | copy-start | bytes 6291460
  7.2 38.4 %copy-start.6 = (s32[3]{0:T(128)S(1)}, s32[3]{0:T(128)}, u32[]{:S(2)}) copy-start(s32[3]{0:T(128)} %param.12) | copy-start | bytes 40
  168.2 1.6 copy-start
  277.1 46.2 %all-to-all-start.3 = ((f32[1,256,4,512]{3,2,0,1:T(4,128)}), f32[1,256,4,512]{3,2,0,1:T(4,128)}, u32[]{:S(2)}, u32[]{:S(2)}) async-start(f32[1,256,4,512]{3,2,0,1:T(4,128)} %copy.82), calls=%async_computation.3 | async-start | bytes 4194304 | tf_op jit(solution)/shard_map/all_to_all | solution.py:31
  282.1 68.7 %all-reduce.2.cloned.1.call-start = ((), (), s32[]{:S(2)}) async-start(), calls=%async_computation.6 | async-start | bytes 4194304 | tf_op jit(solution)/shard_map/psum | solution.py:54
  286.5 0.7 copy-start.7
  286.5 1.2 copy-start.8
  325.6 1.3 copy-start.2
  428.8 74.1 %all-to-all-start.5 = ((f32[1,256,4,512]{3,2,0,1:T(4,128)}), f32[1,256,4,512]{3,2,0,1:T(4,128)}, u32[]{:S(2)}, u32[]{:S(2)}) async-start(f32[1,256,4,512]{3,2,0,1:T(4,128)} %copy.89), calls=%async_computation.5 | async-start | bytes 4194304 | tf_op jit(solution)/shard_map/all_to_all | solution.py:31
  436.4 1.6 copy-start.3
  436.4 2.2 copy-start.4
  505.1 1.6 copy-start.1
Sparse Core Ops, SparseCore 0:
  286.6 64.1 all-reduce.1
where the time goes:
time: 528 us; the launch traced here: 519 us
  blocking collectives  335 us (63%)
  waiting for transfers between devices  56.7 us (11%)
  matrix products  40.5 us (8%)
  local copies, waits for them, and re-layouts  35.2 us (7%)
  other arithmetic  26.4 us (5%)
  between operations  14.5 us (3%)
  starting transfers between devices  10.4 us (2%)
    all_to_all x3, blocking collectives, gaussian_blur_slabs(): lax.all_to_all(section, 'slab', split_axis=2, concat_axis=1, tiled=True)  153 us
    psum x1, blocking collectives, body(): weight_grad = lax.psum(spread_sums, ('atom', 'slab')) / all_cells  60.2 us
    all_to_all x1, blocking collectives, gaussian_blur_slabs(): lax.all_to_all(blurred, 'slab', split_axis=1, concat_axis=2, tiled=True)  52.7 us
    pmax x1, blocking collectives, body(): peak_gradient = lax.pmax(jnp.max(prior_log_scaling, axis=(1, 2, 3)), 'slab')  35.5 us
    all_to_all x2, waiting for transfers between devices, gaussian_blur_slabs(): lax.all_to_all(blurred, 'slab', split_axis=1, concat_axis=2, tiled=True)  34.3 us
    pmax x1, blocking collectives, body(): peak_f = lax.pmax(jnp.max(potential, axis=(1, 2, 3)), 'slab')  33.7 us
    psum x1, waiting for transfers between devices, body(): lax.psum(jnp.sum(atom_cotangent_rows, axis=0), 'atom')  22.4 us
    dot_general x3, matrix products, gaussian_blur_slabs(): jnp.einsum('pq,aqyx->apyx', kern_z, lax.all_to_all(section, 'slab', split...  16.6 us
  transfers between devices with their start and end apart: 3, of which 2 were waited for; matrix products, arithmetic and copies ran while one was open for 3% of the time, Pallas kernels for 0%

commit v1 on v0

v1 whole, which is shorter than its diff:
```python
import functools

import jax
import jax.numpy as jnp
from jax import lax
from jax.experimental import pallas as pl
from jax.experimental.pallas import tpu as pltpu
from jax.sharding import PartitionSpec as P

BAND_MAX = 8
ROWS = 16
MESH = pl.DeviceIdType.MESH
F32 = jnp.float32
BF16 = jnp.bfloat16


def tap(offset):
    spread = offset.astype(F32)
    return jnp.exp(-2.0 * spread * spread / (BAND_MAX * BAND_MAX))


def split(value):
    high = value.astype(BF16)
    return high, (value - high.astype(F32)).astype(BF16)


def dot3(a_high, a_low, b_high, b_low):
    dot = functools.partial(jnp.dot, preferred_element_type=F32)
    return dot(a_high, b_high) + (dot(a_high, b_low) + dot(a_low, b_high))


def kernel(
    swap, slabs, planes, rows, cols,
    dens_hbm, prior_hbm, cot_hbm, bary_hbm, weights_ref, band_ref, slot_ref,
    out_hbm, part_ref,
    own, halo, cot, bary, other, xbuf, zbuf, ybuf, obuf, mine, msg, kx, ky, zmax,
    load_sem, out_sem, hsend, hrecv, msend, mrecv, csend, crecv,
):
    chunks = rows // ROWS
    me = lax.axis_index("slab")
    atom = lax.axis_index("atom")
    right = lax.rem(me + 1, slabs)
    left = lax.rem(me + slabs - 1, slabs)
    has_left = me > 0
    has_right = me < slabs - 1

    loads = [
        pltpu.make_async_copy(src, dst, load_sem.at[i])
        for i, (src, dst) in enumerate(
            [
                (prior_hbm.at[0], own.at[0]),
                (dens_hbm.at[0], own.at[1]),
                (cot_hbm.at[0], cot),
                (bary_hbm, bary),
            ]
        )
    ]
    for load in loads:
        load.start()

    barrier = pltpu.get_barrier_semaphore()

    @pl.when(has_left)
    def _():
        pl.semaphore_signal(barrier, inc=1, device_id=(atom, left), device_id_type=MESH)

    @pl.when(has_right)
    def _():
        pl.semaphore_signal(barrier, inc=1, device_id=(atom, right), device_id_type=MESH)

    if swap:
        pl.semaphore_signal(barrier, inc=1, device_id=(1 - atom, me), device_id_type=MESH)

    def rows_of(c):
        return pl.ds(pl.multiple_of(c * ROWS, ROWS), ROWS)

    def halo_copy(stage, way, c):
        first = planes - BAND_MAX if way == 0 else 0
        return pltpu.make_async_remote_copy(
            src_ref=own.at[stage, pl.ds(first, BAND_MAX), rows_of(c), :],
            dst_ref=halo.at[stage, way, :, rows_of(c), :],
            send_sem=hsend.at[stage, way, c],
            recv_sem=hrecv.at[stage, way, c],
            device_id=(atom, right if way == 0 else left),
            device_id_type=MESH,
        )

    def msg_copy(stage, way):
        return pltpu.make_async_remote_copy(
            src_ref=mine.at[stage],
            dst_ref=msg.at[stage, way],
            send_sem=msend.at[stage, way],
            recv_sem=mrecv.at[stage, way],
            device_id=(atom, right if way == 0 else left),
            device_id_type=MESH,
        )

    def cot_copy(c):
        return pltpu.make_async_remote_copy(
            src_ref=cot_hbm.at[0, :, rows_of(c), :],
            dst_ref=other.at[:, rows_of(c), :],
            send_sem=csend.at[c],
            recv_sem=crecv.at[c],
            device_id=(1 - atom, me),
            device_id_type=MESH,
        )

    there = (has_right, has_left)
    comes = (has_left, has_right)

    def send(stage, c):
        for way in range(2):
            @pl.when(there[way])
            def _():
                halo_copy(stage, way, c).start()

    def send_msg(stage, value):
        mine[stage] = jnp.full((8, 128), value, F32)
        for way in range(2):
            @pl.when(there[way])
            def _():
                msg_copy(stage, way).start()

    def take_msg(stage):
        for way in range(2):
            @pl.when(comes[way])
            def _():
                msg_copy(stage, way).wait_recv()

            @pl.when(jnp.logical_not(comes[way]))
            def _():
                msg[stage, way] = mine[stage]
        return jnp.max(msg[stage, 0]), jnp.max(msg[stage, 1])

    d = lax.broadcasted_iota(jnp.int32, (cols, cols), 0) - lax.broadcasted_iota(jnp.int32, (cols, cols), 1)
    kx[0], kx[1] = split(jnp.where(jnp.abs(d) <= band_ref[0], tap(d), 0.0))
    i = lax.broadcasted_iota(jnp.int32, (8 * ROWS, 16 * ROWS), 0)
    j = lax.broadcasted_iota(jnp.int32, (8 * ROWS, 16 * ROWS), 1)
    d = (j & (2 * ROWS - 1)) - ROWS // 2 - (i & (ROWS - 1))
    same = (i // ROWS) == (j // (2 * ROWS))
    ky[0], ky[1] = split(jnp.where(same & (jnp.abs(d) <= band_ref[1]), tap(d), 0.0))
    xbuf[:, 0:8, :] = jnp.zeros((planes, 8, cols), F32)
    xbuf[:, rows + 8 : rows + 16, :] = jnp.zeros((planes, 8, cols), F32)
    part_ref[...] = jnp.zeros(part_ref.shape, F32)
    for way in range(2):
        @pl.when(jnp.logical_not(comes[way]))
        def _():
            @pl.loop(0, 3)
            def _(stage):
                @pl.loop(0, BAND_MAX)
                def _(p):
                    halo[stage, way, p] = jnp.zeros((rows, cols), F32)

    half = band_ref[2]
    wz = [
        jnp.where(half >= k, tap(jnp.full((8, 128), k, jnp.int32)), 0.0)
        for k in range(BAND_MAX + 1)
    ]

    def zx(stage, c, factors):
        for way in range(2):
            @pl.when(comes[way])
            def _():
                halo_copy(stage, way, c).wait_recv()

        tiles = cols // 128

        @pl.loop(0, tiles * (ROWS // 8))
        def _(t):
            r = pl.multiple_of((t // tiles) * 8, 8)
            at = pl.ds(pl.multiple_of(c * ROWS + r, 8), 8)
            lanes = pl.ds(pl.multiple_of((t % tiles) * 128, 128), 128)
            e = [halo[stage, 0, p, at, lanes] * factors[0] for p in range(BAND_MAX)]
            e += [own[stage, p, at, lanes] * factors[1] for p in range(planes)]
            e += [halo[stage, 1, p, at, lanes] * factors[2] for p in range(BAND_MAX)]
            for p in range(planes):
                total = e[p + 8] * wz[0]
                for k in range(1, BAND_MAX + 1):
                    total = total + (e[p + 8 - k] + e[p + 8 + k]) * wz[k]
                zbuf[p, pl.ds(r, 8), lanes] = total

        high, low = split(zbuf[...].reshape(planes * ROWS, cols))
        res = dot3(high, low, kx[0], kx[1]).reshape(planes, ROWS, cols)
        xbuf[:, pl.ds(pl.multiple_of(c * ROWS + 8, 8), ROWS), :] = res

    def yy(c):
        around = pl.ds(pl.multiple_of(c * ROWS, ROWS), 2 * ROWS)
        for part in range(planes // 8):
            high, low = split(xbuf[part * 8 : part * 8 + 8, around, :].reshape(16 * ROWS, cols))
            ybuf[part * 8 : part * 8 + 8] = dot3(ky[0], ky[1], high, low).reshape(8, ROWS, cols)

    def run(stage, factors, post):
        @pl.loop(0, chunks + 1)
        def _(c):
            @pl.when(c < chunks)
            def _():
                zx(stage, c, factors)

            @pl.when(c > 0)
            def _():
                yy(c - 1)
                post(c - 1)

    def factor(a, b):
        return jnp.exp(jnp.full((8, 128), a - b, F32))

    loads[0].wait()
    zmax[...] = jnp.full((8, cols), -jnp.inf, F32)

    @pl.loop(0, planes)
    def _(p):
        zmax[...] = jnp.maximum(zmax[...], jnp.max(own[0, p].reshape(rows // 8, 8, cols), axis=0))

    m1 = jnp.max(zmax[...])
    count = has_left.astype(jnp.int32) + has_right.astype(jnp.int32) + (1 if swap else 0)
    pl.semaphore_wait(barrier, count)
    send_msg(0, m1)

    @pl.loop(0, chunks)
    def _(c):
        @pl.loop(0, planes)
        def _(p):
            own[0, p, rows_of(c), :] = jnp.exp(own[0, p, rows_of(c), :] - m1)

        send(0, c)

    if swap:
        @pl.loop(0, chunks)
        def _(c):
            cot_copy(c).start()

    m1_left, m1_right = take_msg(0)
    c1 = jnp.maximum(m1, jnp.maximum(m1_left, m1_right))
    loads[1].wait()
    zmax[...] = jnp.full((8, cols), -jnp.inf, F32)

    def post1(c):
        @pl.loop(0, planes)
        def _(p):
            potential = own[1, p, rows_of(c), :] - (jnp.log(ybuf[p]) + c1)
            own[1, p, rows_of(c), :] = potential
            zmax[...] = jnp.maximum(zmax[...], jnp.max(potential.reshape(ROWS // 8, 8, cols), axis=0))

    run(0, [factor(m1_left, c1), factor(m1, c1), factor(m1_right, c1)], post1)

    m2 = jnp.max(zmax[...])
    send_msg(1, m2)

    @pl.loop(0, chunks)
    def _(c):
        @pl.loop(0, planes)
        def _(p):
            own[1, p, rows_of(c), :] = jnp.exp(own[1, p, rows_of(c), :] - m2)

        send(1, c)

    m2_left, m2_right = take_msg(1)
    c2 = jnp.maximum(m2, jnp.maximum(m2_left, m2_right))
    send_msg(2, c2)
    weight = weights_ref[slot_ref[atom]]
    loads[2].wait()
    loads[3].wait()

    def post2(c):
        if swap:
            cot_copy(c).wait_recv()

        @pl.loop(0, planes)
        def _(p):
            cot_here = cot[p, rows_of(c), :]
            summed = bary[p, rows_of(c), :]
            if swap:
                summed = summed + (cot_here + other[p, rows_of(c), :])
            second = ybuf[p]
            product = summed * (jnp.log(second) + c2)
            part_ref[...] += jnp.sum(product.reshape(ROWS // 8, 8, cols), axis=0)
            own[2, p, rows_of(c), :] = (weight * summed - cot_here) / second

        send(2, c)

    run(1, [factor(m2_left, c2), factor(m2, c2), factor(m2_right, c2)], post2)

    c2_left, c2_right = take_msg(2)

    def out_copy(c):
        return pltpu.make_async_copy(
            obuf.at[:, rows_of(c), :], out_hbm.at[0, :, rows_of(c), :], out_sem.at[c]
        )

    def post3(c):
        @pl.loop(0, planes)
        def _(p):
            obuf[p, rows_of(c), :] = own[1, p, rows_of(c), :] * ybuf[p]

        out_copy(c).start()

    run(2, [factor(m2, c2_left), factor(m2, c2), factor(m2, c2_right)], post3)

    @pl.loop(0, chunks)
    def _(c):
        out_copy(c).wait()
        if swap:
            cot_copy(c).wait_send()
        for stage in range(3):
            for way in range(2):
                @pl.when(there[way])
                def _():
                    halo_copy(stage, way, c).wait_send()

    for stage in range(3):
        for way in range(2):
            @pl.when(there[way])
            def _():
                msg_copy(stage, way).wait_send()


def body(dens, prior, cot, bary, weights, band, slot_atom_index):
    held = dens.shape[0]
    assert held == 1
    planes, rows, cols = bary.shape
    slabs = lax.axis_size("slab")
    swap = lax.axis_size("atom") == 2
    chunks = rows // ROWS
    if not swap:
        bary = bary + lax.psum(cot[0], "atom")
    dma = pltpu.SemaphoreType.DMA
    full = pltpu.VMEM((planes, rows, cols), F32)
    grad, part = pl.pallas_call(
        functools.partial(kernel, swap, slabs, planes, rows, cols),
        out_shape=(
            jax.ShapeDtypeStruct(dens.shape, F32),
            jax.ShapeDtypeStruct((8, cols), F32),
        ),
        in_specs=[pl.BlockSpec(memory_space=pl.ANY)] * 4 + [pl.BlockSpec(memory_space=pltpu.SMEM)] * 3,
        out_specs=(pl.BlockSpec(memory_space=pl.ANY), pl.BlockSpec(memory_space=pltpu.VMEM)),
        scratch_shapes=[
            pltpu.VMEM((3, planes, rows, cols), F32),
            pltpu.VMEM((3, 2, BAND_MAX, rows, cols), F32),
            full,
            full,
            full,
            pltpu.VMEM((planes, rows + 16, cols), F32),
            pltpu.VMEM((planes, ROWS, cols), F32),
            pltpu.VMEM((planes, ROWS, cols), F32),
            full,
            pltpu.VMEM((3, 8, 128), F32),
            pltpu.VMEM((3, 2, 8, 128), F32),
            pltpu.VMEM((2, cols, cols), BF16),
            pltpu.VMEM((2, 8 * ROWS, 16 * ROWS), BF16),
            pltpu.VMEM((8, cols), F32),
            dma((4,)),
            dma((chunks,)),
            dma((3, 2, chunks)),
            dma((3, 2, chunks)),
            dma((3, 2)),
            dma((3, 2)),
            dma((chunks,)),
            dma((chunks,)),
        ],
        compiler_params=pltpu.CompilerParams(
            collective_id=0, has_side_effects=True, vmem_limit_bytes=52 * 1024 * 1024
        ),
        name="sinkhorn_reverse",
    )(dens, prior, cot, bary, weights, band, slot_atom_index)
    atom = lax.axis_index("atom")
    slot = lax.dynamic_slice_in_dim(slot_atom_index, atom, 1)
    onehot = (slot == jnp.arange(weights.shape[0], dtype=jnp.int32)).astype(F32)
    weight_grad = lax.psum(onehot * jnp.sum(part), ("atom", "slab")) / (slabs * planes * rows * cols)
    return grad, weight_grad


def solution(mesh):
    return jax.shard_map(
        body,
        mesh=mesh,
        in_specs=(
            P("atom", "slab", None, None),
            P("atom", "slab", None, None),
            P("atom", "slab", None, None),
            P("slab", None, None),
            P(),
            P(),
            P(),
        ),
        out_specs=(P("atom", "slab", None, None), P()),
        check_vma=False,
    )
```

time: 528 us -> 132 us (0.25); the launches traced: 519 us -> 132 us
  blocking collectives: 335 us -> 58 us
  Pallas kernels: 0 us -> 64.6 us
  waiting for transfers between devices: 56.7 us -> 0 us
  matrix products: 40.5 us -> 0 us
  local copies, waits for them, and re-layouts: 35.2 us -> 6.35 us
  other arithmetic: 26.4 us -> 2.41 us
  between operations: 14.5 us -> 0.65 us
  starting transfers between devices: 10.4 us -> 0 us
    all_to_all x4 -> x0, blocking collectives: 205 us -> none  [the longest x3 153 us: gaussian_blur_slabs(): lax.all_to_all(section, 'slab', split_axis=2, concat_axis=1, tiled=True)]
    pmax x2 -> x0, blocking collectives: 69.2 us -> none  [the longest x1 35.5 us: body(): peak_gradient = lax.pmax(jnp.max(prior_log_scaling, axis=(1, 2, 3)), 'slab')]
    pallas_call x0 -> x1, Pallas kernels: none -> 64.6 us  [body(): pl.pallas_call(functools.partial(kernel, swap, slabs, planes, rows, cols)...]
    dot_general x9 -> x0, matrix products: 40.5 us -> none  [the longest x3 16.6 us: gaussian_blur_slabs(): jnp.einsum('pq,aqyx->apyx', kern_z, lax.all_to_all(section, 'slab', split...]
    all_to_all x2 -> x0, waiting for transfers between devices: 34.3 us -> none  [gaussian_blur_slabs(): lax.all_to_all(blurred, 'slab', split_axis=1, concat_axis=2, tiled=True)]
    psum x1 -> x0, waiting for transfers between devices: 22.4 us -> none  [body(): lax.psum(jnp.sum(atom_cotangent_rows, axis=0), 'atom')]
    transpose x6 -> x0, local copies, waits for them, and re-layouts: 13 us -> none  [the longest x3 9.17 us: gaussian_blur_slabs(): jnp.einsum('pq,aqyx->apyx', kern_z, lax.all_to_all(section, 'slab', split...]
    another operation x2 -> x0, other arithmetic: 10.4 us -> none
  transfers between devices with their start and end apart: 3 -> 0, of which waited for: 2 -> 0; matrix products, arithmetic and copies ran while one was open for 3% -> 0% of each run, Pallas kernels for 0% -> 0%
where the time goes in v1:
time: 132 us
  Pallas kernels  64.6 us (49%)
  blocking collectives  58 us (44%)
  local copies, waits for them, and re-layouts  6.35 us (5%)
  other arithmetic  2.41 us (2%)
    pallas_call x1, Pallas kernels, body(): pl.pallas_call(functools.partial(kernel, swap, slabs, planes, rows, cols)...  64.6 us
    psum x1, blocking collectives, body(): lax.psum(onehot * jnp.sum(part), ('atom', 'slab'))  58 us
    unnamed x7, local copies, waits for them, and re-layouts  5.11 us

profile of v1, /device:TPU:0, one launch (start us, length us, event | category | flops | bytes accessed | tf_op | source)
XLA Modules:
  0.0 132.0 jit_solution(13797222203534530732)
XLA Ops:
  0.6 1.2 dynamic_slice.3
  1.9 0.0 copy-start
  1.9 0.7 copy-done
  2.5 0.0 copy-start.1
  2.5 0.7 copy-done.1
  3.2 0.0 copy-start.2
  3.2 0.7 copy-done.2
  3.8 64.6 %sinkhorn_reverse.1 = (f32[1,16,64,512]{3,2,1,0:T(8,128)}, f32[8,512]{1,0:T(8,128)S(1)}) custom-call(f32[1,16,64,512]{3,2,1,0:T(8,128)} %dens_hbm.1, f32[1,16,64,512]{3,2,1,0:T(8,128)} %prior_hbm.1, f32[1,16,64,512]{3,2,1,0:T(8,128)} %cot_hbm.1, f32[16,64,512]{2,1,0:T(8,128)} %bary_hbm.1, f32[2]{0:T(128)S(1)} %copy-done, s32[3]{0:T(128)S(1)} %copy-done.1, ...), custom_call_target="tpu_custom_call" | custom-call | tf_op jit(solution)/shard_map/sinkhorn_reverse/pallas_call | solution.py:328
  68.5 0.6 reduce_sum.9
  69.1 1.3 compare_select_fusion
  70.4 58.0 %psum.7 = f32[2]{0:T(128)S(1)} all-reduce(f32[2]{0:T(128)S(1)} %compare_select_fusion), channel_id=1, replica_groups=mesh['atom'=2,'slab'=16] {'atom','slab'}, use_global_device_ids=true, to_apply=%region_1.0 | all-reduce | flops 2 | bytes 16 | tf_op jit(solution)/shard_map/psum | solution.py:368
  128.3 0.5 broadcast_multiply_fusion
  128.8 3.1 %copy.10 = f32[1,16,64,512]{3,2,1,0:T(8,128)} copy(f32[1,16,64,512]{3,2,1,0:T(8,128)} %get-tuple-element.8) | data formatting | bytes 4194304
Async XLA Ops:
  1.9 0.7 copy-start
  2.5 0.7 copy-start.1
  3.2 0.7 copy-start.2

commit v2 on v1

--- a/solution.py
+++ b/solution.py
@@ -30,11 +30,11 @@
 
 
 def kernel(
-    swap, slabs, planes, rows, cols,
+    swap, atoms, slabs, planes, rows, cols,
     dens_hbm, prior_hbm, cot_hbm, bary_hbm, weights_ref, band_ref, slot_ref,
-    out_hbm, part_ref,
-    own, halo, cot, bary, other, xbuf, zbuf, ybuf, obuf, mine, msg, kx, ky, zmax,
-    load_sem, out_sem, hsend, hrecv, msend, mrecv, csend, crecv,
+    out_hbm, wgrad_ref,
+    own, halo, cot, bary, other, xbuf, zbuf, ybuf, obuf, mine, msg, kx, ky, zmax, part_ref, slab_parts, atom_parts,
+    load_sem, out_sem, hsend, hrecv, msend, mrecv, csend, crecv, psend, precv, asend, arecv,
 ):
     chunks = rows // ROWS
     me = lax.axis_index("slab")
@@ -60,16 +60,17 @@
 
     barrier = pltpu.get_barrier_semaphore()
 
-    @pl.when(has_left)
-    def _():
-        pl.semaphore_signal(barrier, inc=1, device_id=(atom, left), device_id_type=MESH)
-
-    @pl.when(has_right)
-    def _():
-        pl.semaphore_signal(barrier, inc=1, device_id=(atom, right), device_id_type=MESH)
-
-    if swap:
-        pl.semaphore_signal(barrier, inc=1, device_id=(1 - atom, me), device_id_type=MESH)
+    @pl.loop(1, slabs)
+    def _(k):
+        pl.semaphore_signal(
+            barrier, inc=1, device_id=(atom, lax.rem(me + k, slabs)), device_id_type=MESH
+        )
+
+    @pl.loop(1, atoms)
+    def _(k):
+        pl.semaphore_signal(
+            barrier, inc=1, device_id=(lax.rem(atom + k, atoms), me), device_id_type=MESH
+        )
 
     def rows_of(c):
         return pl.ds(pl.multiple_of(c * ROWS, ROWS), ROWS)
@@ -102,6 +103,26 @@
             send_sem=csend.at[c],
             recv_sem=crecv.at[c],
             device_id=(1 - atom, me),
+            device_id_type=MESH,
+        )
+
+    def part_copy(source, target):
+        return pltpu.make_async_remote_copy(
+            src_ref=slab_parts.at[me],
+            dst_ref=slab_parts.at[source],
+            send_sem=psend.at[target],
+            recv_sem=precv.at[source],
+            device_id=(atom, target),
+            device_id_type=MESH,
+        )
+
+    def atom_copy(source, target):
+        return pltpu.make_async_remote_copy(
+            src_ref=atom_parts.at[atom],
+            dst_ref=atom_parts.at[source],
+            send_sem=asend.at[target],
+            recv_sem=arecv.at[source],
+            device_id=(target, me),
             device_id_type=MESH,
         )
 
@@ -212,8 +233,7 @@
         zmax[...] = jnp.maximum(zmax[...], jnp.max(own[0, p].reshape(rows // 8, 8, cols), axis=0))
 
     m1 = jnp.max(zmax[...])
-    count = has_left.astype(jnp.int32) + has_right.astype(jnp.int32) + (1 if swap else 0)
-    pl.semaphore_wait(barrier, count)
+    pl.semaphore_wait(barrier, slabs - 1 + atoms - 1)
     send_msg(0, m1)
 
     @pl.loop(0, chunks)
@@ -280,6 +300,24 @@
 
     run(1, [factor(m2_left, c2), factor(m2, c2), factor(m2_right, c2)], post2)
 
+    slab_parts[me] = sum(part_ref[:, k * 128 : (k + 1) * 128] for k in range(cols // 128))
+
+    @pl.loop(1, slabs)
+    def _(k):
+        part_copy(me, lax.rem(me + k, slabs)).start()
+
+    def share():
+        @pl.loop(1, slabs)
+        def _(k):
+            other_slab = lax.rem(me + k, slabs)
+            part_copy(other_slab, other_slab).wait_recv()
+
+        atom_parts[atom] = jnp.sum(slab_parts[...], axis=0) / (slabs * planes * rows * cols)
+
+        @pl.loop(1, atoms)
+        def _(k):
+            atom_copy(atom, lax.rem(atom + k, atoms)).start()
+
     c2_left, c2_right = take_msg(2)
 
     def out_copy(c):
@@ -293,6 +331,10 @@
             obuf[p, rows_of(c), :] = own[1, p, rows_of(c), :] * ybuf[p]
 
         out_copy(c).start()
+
+        @pl.when(c == chunks - 2)
+        def _():
+            share()
 
     run(2, [factor(m2, c2_left), factor(m2, c2), factor(m2, c2_right)], post3)
 
@@ -313,26 +355,42 @@
             def _():
                 msg_copy(stage, way).wait_send()
 
+    @pl.loop(1, slabs)
+    def _(k):
+        target = lax.rem(me + k, slabs)
+        part_copy(me, target).wait_send()
+
+    @pl.loop(1, atoms)
+    def _(k):
+        other_atom = lax.rem(atom + k, atoms)
+        atom_copy(atom, other_atom).wait_send()
+        atom_copy(other_atom, other_atom).wait_recv()
+
+    totals = [jnp.sum(atom_parts[k]) for k in range(atoms)]
+    for j in range(atoms):
+        wgrad_ref[j] = sum(jnp.where(slot_ref[k] == j, totals[k], 0.0) for k in range(atoms))
+
 
 def body(dens, prior, cot, bary, weights, band, slot_atom_index):
     held = dens.shape[0]
     assert held == 1
     planes, rows, cols = bary.shape
     slabs = lax.axis_size("slab")
-    swap = lax.axis_size("atom") == 2
+    atoms = lax.axis_size("atom")
+    swap = atoms == 2
     chunks = rows // ROWS
     if not swap:
         bary = bary + lax.psum(cot[0], "atom")
     dma = pltpu.SemaphoreType.DMA
     full = pltpu.VMEM((planes, rows, cols), F32)
-    grad, part = pl.pallas_call(
-        functools.partial(kernel, swap, slabs, planes, rows, cols),
+    return pl.pallas_call(
+        functools.partial(kernel, swap, atoms, slabs, planes, rows, cols),
         out_shape=(
             jax.ShapeDtypeStruct(dens.shape, F32),
-            jax.ShapeDtypeStruct((8, cols), F32),
+            jax.ShapeDtypeStruct((atoms,), F32),
         ),
         in_specs=[pl.BlockSpec(memory_space=pl.ANY)] * 4 + [pl.BlockSpec(memory_space=pltpu.SMEM)] * 3,
-        out_specs=(pl.BlockSpec(memory_space=pl.ANY), pl.BlockSpec(memory_space=pltpu.VMEM)),
+        out_specs=(pl.BlockSpec(memory_space=pl.ANY), pl.BlockSpec(memory_space=pltpu.SMEM)),
         scratch_shapes=[
             pltpu.VMEM((3, planes, rows, cols), F32),
             pltpu.VMEM((3, 2, BAND_MAX, rows, cols), F32),
@@ -348,6 +406,9 @@
             pltpu.VMEM((2, cols, cols), BF16),
             pltpu.VMEM((2, 8 * ROWS, 16 * ROWS), BF16),
             pltpu.VMEM((8, cols), F32),
+            pltpu.VMEM((8, cols), F32),
+            pltpu.VMEM((slabs, 8, 128), F32),
+            pltpu.VMEM((atoms, 8, 128), F32),
             dma((4,)),
             dma((chunks,)),
             dma((3, 2, chunks)),
@@ -356,17 +417,16 @@
             dma((3, 2)),
             dma((chunks,)),
             dma((chunks,)),
+            dma((slabs,)),
+            dma((slabs,)),
+            dma((atoms,)),
+            dma((atoms,)),
         ],
         compiler_params=pltpu.CompilerParams(
             collective_id=0, has_side_effects=True, vmem_limit_bytes=52 * 1024 * 1024
         ),
         name="sinkhorn_reverse",
     )(dens, prior, cot, bary, weights, band, slot_atom_index)
-    atom = lax.axis_index("atom")
-    slot = lax.dynamic_slice_in_dim(slot_atom_index, atom, 1)
-    onehot = (slot == jnp.arange(weights.shape[0], dtype=jnp.int32)).astype(F32)
-    weight_grad = lax.psum(onehot * jnp.sum(part), ("atom", "slab")) / (slabs * planes * rows * cols)
-    return grad, weight_grad
 
 
 def solution(mesh):

time: 132 us -> 92.4 us (0.70)
  the two profiles are of different devices: /device:TPU:0 before, /device:TPU:9 now
where the time goes in v2:
time: 92.4 us; the launch traced here: 92.3 us
  Pallas kernels  86 us (93%)
  local copies, waits for them, and re-layouts  5.61 us (6%)
    pallas_call x1, Pallas kernels, body(): pl.pallas_call(functools.partial(kernel, swap, atoms, slabs, planes, rows...  86 us
    unnamed x8, local copies, waits for them, and re-layouts  5.61 us

profile of v2, /device:TPU:9, one launch (start us, length us, event | category | flops | bytes accessed | tf_op | source)
XLA Modules:
  0.0 92.3 jit_solution(18419116014159589334)
XLA Ops:
  0.6 0.0 copy-start
  0.6 0.6 copy-done
  1.3 0.0 copy-start.1
  1.3 0.7 copy-done.1
  1.9 0.0 copy-start.2
  1.9 0.7 copy-done.2
  2.6 86.0 %sinkhorn_reverse.1 = (f32[1,16,64,512]{3,2,1,0:T(8,128)}, f32[2]{0:T(128)S(1)}) custom-call(f32[1,16,64,512]{3,2,1,0:T(8,128)} %dens_hbm.1, f32[1,16,64,512]{3,2,1,0:T(8,128)} %prior_hbm.1, f32[1,16,64,512]{3,2,1,0:T(8,128)} %cot_hbm.1, f32[16,64,512]{2,1,0:T(8,128)} %bary_hbm.1, f32[2]{0:T(128)S(1)} %copy-done, s32[3]{0:T(128)S(1)} %copy-done.1, ...), custom_call_target="tpu_custom_call" | custom-call | tf_op jit(solution)/shard_map/sinkhorn_reverse/pallas_call | solution.py:386
  88.6 3.1 %copy.11 = f32[1,16,64,512]{3,2,1,0:T(8,128)} copy(f32[1,16,64,512]{3,2,1,0:T(8,128)} %get-tuple-element.4) | data formatting | bytes 4194304
  91.8 0.5 copy.12
Async XLA Ops:
  0.6 0.7 copy-start
  1.3 0.7 copy-start.1
  1.9 0.7 copy-start.2

commit v3 on v2

--- a/solution.py
+++ b/solution.py
@@ -9,6 +9,7 @@
 
 BAND_MAX = 8
 ROWS = 16
+STEP = 2
 MESH = pl.DeviceIdType.MESH
 F32 = jnp.float32
 BF16 = jnp.bfloat16
@@ -30,10 +31,11 @@
 
 
 def kernel(
-    swap, atoms, slabs, planes, rows, cols,
-    dens_hbm, prior_hbm, cot_hbm, bary_hbm, weights_ref, band_ref, slot_ref,
+    reach, swap, atoms, slabs, planes, rows, cols,
+    dens_hbm, prior_hbm, cot_hbm, bary_hbm, weights_hbm, band_hbm, slot_hbm,
     out_hbm, wgrad_ref,
     own, halo, cot, bary, other, xbuf, zbuf, ybuf, obuf, mine, msg, kx, ky, zmax, part_ref, slab_parts, atom_parts,
+    weights_ref, band_ref, slot_ref,
     load_sem, out_sem, hsend, hrecv, msend, mrecv, csend, crecv, psend, precv, asend, arecv,
 ):
     chunks = rows // ROWS
@@ -48,6 +50,9 @@
         pltpu.make_async_copy(src, dst, load_sem.at[i])
         for i, (src, dst) in enumerate(
             [
+                (band_hbm, band_ref),
+                (weights_hbm, weights_ref),
+                (slot_hbm, slot_ref),
                 (prior_hbm.at[0], own.at[0]),
                 (dens_hbm.at[0], own.at[1]),
                 (cot_hbm.at[0], cot),
@@ -76,9 +81,9 @@
         return pl.ds(pl.multiple_of(c * ROWS, ROWS), ROWS)
 
     def halo_copy(stage, way, c):
-        first = planes - BAND_MAX if way == 0 else 0
+        first = planes - reach if way == 0 else 0
         return pltpu.make_async_remote_copy(
-            src_ref=own.at[stage, pl.ds(first, BAND_MAX), rows_of(c), :],
+            src_ref=own.at[stage, pl.ds(first, reach), rows_of(c), :],
             dst_ref=halo.at[stage, way, :, rows_of(c), :],
             send_sem=hsend.at[stage, way, c],
             recv_sem=hrecv.at[stage, way, c],
@@ -152,6 +157,9 @@
             def _():
                 msg[stage, way] = mine[stage]
         return jnp.max(msg[stage, 0]), jnp.max(msg[stage, 1])
+
+    for load in loads[:3]:
+        load.wait()
 
     d = lax.broadcasted_iota(jnp.int32, (cols, cols), 0) - lax.broadcasted_iota(jnp.int32, (cols, cols), 1)
     kx[0], kx[1] = split(jnp.where(jnp.abs(d) <= band_ref[0], tap(d), 0.0))
@@ -168,14 +176,14 @@
         def _():
             @pl.loop(0, 3)
             def _(stage):
-                @pl.loop(0, BAND_MAX)
+                @pl.loop(0, reach)
                 def _(p):
                     halo[stage, way, p] = jnp.zeros((rows, cols), F32)
 
     half = band_ref[2]
     wz = [
         jnp.where(half >= k, tap(jnp.full((8, 128), k, jnp.int32)), 0.0)
-        for k in range(BAND_MAX + 1)
+        for k in range(reach + 1)
     ]
 
     def zx(stage, c, factors):
@@ -191,13 +199,13 @@
             r = pl.multiple_of((t // tiles) * 8, 8)
             at = pl.ds(pl.multiple_of(c * ROWS + r, 8), 8)
             lanes = pl.ds(pl.multiple_of((t % tiles) * 128, 128), 128)
-            e = [halo[stage, 0, p, at, lanes] * factors[0] for p in range(BAND_MAX)]
+            e = [halo[stage, 0, p, at, lanes] * factors[0] for p in range(reach)]
             e += [own[stage, p, at, lanes] * factors[1] for p in range(planes)]
-            e += [halo[stage, 1, p, at, lanes] * factors[2] for p in range(BAND_MAX)]
+            e += [halo[stage, 1, p, at, lanes] * factors[2] for p in range(reach)]
             for p in range(planes):
-                total = e[p + 8] * wz[0]
-                for k in range(1, BAND_MAX + 1):
-                    total = total + (e[p + 8 - k] + e[p + 8 + k]) * wz[k]
+                total = e[p + reach] * wz[0]
+                for k in range(1, reach + 1):
+                    total = total + (e[p + reach - k] + e[p + reach + k]) * wz[k]
                 zbuf[p, pl.ds(r, 8), lanes] = total
 
         high, low = split(zbuf[...].reshape(planes * ROWS, cols))
@@ -225,7 +233,7 @@
     def factor(a, b):
         return jnp.exp(jnp.full((8, 128), a - b, F32))
 
-    loads[0].wait()
+    loads[3].wait()
     zmax[...] = jnp.full((8, cols), -jnp.inf, F32)
 
     @pl.loop(0, planes)
@@ -251,7 +259,7 @@
 
     m1_left, m1_right = take_msg(0)
     c1 = jnp.maximum(m1, jnp.maximum(m1_left, m1_right))
-    loads[1].wait()
+    loads[4].wait()
     zmax[...] = jnp.full((8, cols), -jnp.inf, F32)
 
     def post1(c):
@@ -278,8 +286,8 @@
     c2 = jnp.maximum(m2, jnp.maximum(m2_left, m2_right))
     send_msg(2, c2)
     weight = weights_ref[slot_ref[atom]]
-    loads[2].wait()
-    loads[3].wait()
+    loads[5].wait()
+    loads[6].wait()
 
     def post2(c):
         if swap:
@@ -372,6 +380,19 @@
 
 
 def body(dens, prior, cot, bary, weights, band, slot_atom_index):
+    swap = lax.axis_size("atom") == 2
+    if not swap:
+        bary = bary + lax.psum(cot[0], "atom")
+    steps = BAND_MAX // STEP
+    which = sum((band[2] > STEP * k).astype(jnp.int32) for k in range(1, steps))
+    return lax.switch(
+        which,
+        [functools.partial(reverse, STEP * (k + 1)) for k in range(steps)],
+        dens, prior, cot, bary, weights, band, slot_atom_index,
+    )
+
+
+def reverse(reach, dens, prior, cot, bary, weights, band, slot_atom_index):
     held = dens.shape[0]
     assert held == 1
     planes, rows, cols = bary.shape
@@ -379,21 +400,19 @@
     atoms = lax.axis_size("atom")
     swap = atoms == 2
     chunks = rows // ROWS
-    if not swap:
-        bary = bary + lax.psum(cot[0], "atom")
     dma = pltpu.SemaphoreType.DMA
     full = pltpu.VMEM((planes, rows, cols), F32)
     return pl.pallas_call(
-        functools.partial(kernel, swap, atoms, slabs, planes, rows, cols),
+        functools.partial(kernel, reach, swap, atoms, slabs, planes, rows, cols),
         out_shape=(
             jax.ShapeDtypeStruct(dens.shape, F32),
             jax.ShapeDtypeStruct((atoms,), F32),
         ),
-        in_specs=[pl.BlockSpec(memory_space=pl.ANY)] * 4 + [pl.BlockSpec(memory_space=pltpu.SMEM)] * 3,
+        in_specs=[pl.BlockSpec(memory_space=pl.ANY)] * 7,
         out_specs=(pl.BlockSpec(memory_space=pl.ANY), pl.BlockSpec(memory_space=pltpu.SMEM)),
         scratch_shapes=[
             pltpu.VMEM((3, planes, rows, cols), F32),
-            pltpu.VMEM((3, 2, BAND_MAX, rows, cols), F32),
+            pltpu.VMEM((3, 2, reach, rows, cols), F32),
             full,
             full,
             full,
@@ -409,7 +428,10 @@
             pltpu.VMEM((8, cols), F32),
             pltpu.VMEM((slabs, 8, 128), F32),
             pltpu.VMEM((atoms, 8, 128), F32),
-            dma((4,)),
+            pltpu.SMEM((atoms,), F32),
+            pltpu.SMEM((3,), jnp.int32),
+            pltpu.SMEM((atoms,), jnp.int32),
+            dma((7,)),
             dma((chunks,)),
             dma((3, 2, chunks)),
             dma((3, 2, chunks)),
@@ -423,9 +445,9 @@
             dma((atoms,)),
         ],
         compiler_params=pltpu.CompilerParams(
-            collective_id=0, has_side_effects=True, vmem_limit_bytes=52 * 1024 * 1024
+            collective_id=reach, has_side_effects=True, vmem_limit_bytes=52 * 1024 * 1024
         ),
-        name="sinkhorn_reverse",
+        name=f"sinkhorn_reach_{reach}",
     )(dens, prior, cot, bary, weights, band, slot_atom_index)
 
 

time: 92.4 us -> 74.3 us (0.80)
  Pallas kernels: 86 us -> 68.4 us
  local copies, waits for them, and re-layouts: 5.61 us -> 3.07 us
  between operations: 0.65 us -> 2.59 us
    pallas_call x1, Pallas kernels: 86 us -> 68.4 us  [reverse(): pl.pallas_call(functools.partial(kernel, reach, swap, atoms, slabs, plane...]
    unnamed x8 -> x2, local copies, waits for them, and re-layouts: 5.61 us -> 1.83 us
    slice x0 -> x1, local copies, waits for them, and re-layouts: none -> 1.24 us  [body(): band[2] > STEP * k]
where the time goes in v3:
time: 74.3 us; the launch traced here: 74.1 us
  Pallas kernels  68.4 us (92%)
  local copies, waits for them, and re-layouts  3.07 us (4%)
  between operations  2.59 us (3%)
    pallas_call x1, Pallas kernels, reverse(): pl.pallas_call(functools.partial(kernel, reach, swap, atoms, slabs, plane...  68.4 us
    unnamed x2, local copies, waits for them, and re-layouts  1.83 us

profile of v3, /device:TPU:9, one launch (start us, length us, event | category | flops | bytes accessed | tf_op | source)
XLA Modules:
  0.0 74.1 jit_solution(8570177813172889814)
XLA Ops:
  0.6 1.2 %slice.2 = s32[1]{0:T(128)} slice(s32[3]{0:T(128)} %param.16), slice={[2:3]} | slice | bytes 8 | tf_op jit(solution)/shard_map/slice | solution.py:387
  3.8 68.5 %conditional.1 = ((f32[1,16,64,512]{3,2,1,0:T(8,128)S(1)}, f32[2]{0:T(128)S(1)})) conditional(s32[]{:T(128)} %bitcast, (f32[1,16,64,512]{3,2,1,0:T(8,128)}, f32[1,16,64,512]{3,2,1,0:T(8,128)}, f32[1,16,64,512]{3,2,1,0:T(8,128)}, f32[16,64,512]{2,1,0:T(8,128)}, f32[2]{0:T(128)}, /*index=5*/s32[3]{0:T(128)}, ...), branch_computations={%region_0.0_spmd, %region_1.0_spmd, %region_2.0_spmd, %region_3.0_... | conditional | bytes 8 | solution.py:388
  3.8 68.4 %sinkhorn_reach_6.1 = (f32[1,16,64,512]{3,2,1,0:T(8,128)S(1)}, f32[2]{0:T(128)S(1)}) custom-call(f32[1,16,64,512]{3,2,1,0:T(8,128)} %get-tuple-element.70.dens_hbm, f32[1,16,64,512]{3,2,1,0:T(8,128)} %get-tuple-element.71.prior_hbm, f32[1,16,64,512]{3,2,1,0:T(8,128)} %get-tuple-element.72.cot_hbm, f32[16,64,512]{2,1,0:T(8,128)} %get-tuple-element.73.bary_hbm, ...), custom_call_target="tpu_custom_call" | custom-call | tf_op jit(solution)/shard_map/cond/branch_2_fun/sinkhorn_reach_6/pallas_call | solution.py:405
  72.3 1.3 %copy.27 = f32[1,16,64,512]{3,2,1,0:T(8,128)} copy(f32[1,16,64,512]{3,2,1,0:T(8,128)S(1)} %get-tuple-element.106) | data formatting | bytes 4194304
  73.6 0.5 copy.28
